TPU v7x, 512 devices: a whole 4x4x16 slice. The times are simulated.
512 devices in a mesh: seq: 64 (over x, z_lo, core), head: 8 (over y, z_hi).
Axes of the slice: x: 4, y: 4, z: 16 (z_hi: 2, z_lo: 8; z = z_hi * 8 + z_lo), core: 2. Of those that a mesh axis runs over, the one named last changes fastest.
Arguments:
- queries: bfloat16 [16384, 8192], P(('seq', 'head')), may hold values from -8 to 8
- cache_keys: bfloat16 [4096, 1024], P('seq', 'head'), may hold values from -4 to 4
- cache_values: bfloat16 [4096, 1024], P('seq', 'head'), may hold values from -4 to 4
- slab_keys: bfloat16 [16384, 1024], P('seq', 'head'), may hold values from -4 to 4
- slab_values: bfloat16 [16384, 1024], P('seq', 'head'), may hold values from -4 to 4
- block_lists: int32 [64, 256, 24], P('head', 'seq'), may hold values from 0 to 63, as said below
Outputs:
- attended: bfloat16 [16384, 8192], P(('seq', 'head'))
Inputs may be any that keep to these rules, and one draw needn't show every extreme that they name: `block_lists`: for each head and query block the 24 entries are distinct. Entries 0 to 11 are the head's vertical blocks, the same for all its query blocks, all below 32, the first one 0. Entry 12 + j of query block q is 32 + (o_j + q) mod (32) for the head's own distinct offsets o_j.
All inputs are finite; a program needn't handle non-finite values.
Results may differ from a plain program's by a relative error of at most 0.0049.
Values may be sent and summed in bfloat16 or wider, within the bound.
No kernel may reach another device: no remote copies, remote signals or barrier semaphores. Data moves between devices by JAX's collectives and lax.ppermute only.
A program may use at most 64 MiB of HBM per device.

v0:
```python
import jax
import jax.numpy as jnp
from jax import lax
from jax.sharding import PartitionSpec as P

DH = 128
BLOCK = 64
WIN = 4


def softmax_weights(logit_matrix, allowed):
    masked = jnp.where(allowed, logit_matrix, -jnp.inf)
    highest = jnp.max(masked, axis=-1, keepdims=True)
    raised = jnp.exp(masked - highest)
    return (raised / jnp.sum(raised, axis=-1, keepdims=True)).astype(jnp.bfloat16)


def per_device(queries, cache_keys, cache_values, slab_keys, slab_values, block_lists):
    head_count = block_lists.shape[0]
    blocks_here = block_lists.shape[1]
    listed = block_lists.shape[2]
    kv_count = cache_keys.shape[1] // DH
    group_size = head_count // kv_count
    seq_position = lax.axis_index("seq")
    offsets = jnp.arange(WIN, dtype=jnp.int32)
    query_blocks = seq_position * blocks_here + jnp.arange(blocks_here, dtype=jnp.int32)
    slab_valid = query_blocks[:, None] - offsets[None, :] >= 0
    arrived = lax.all_to_all(queries, "head", split_axis=1, concat_axis=0, tiled=True)
    gathered_keys = lax.all_gather(cache_keys, "seq", axis=0, tiled=True)
    gathered_values = lax.all_gather(cache_values, "seq", axis=0, tiled=True)
    source_keys = lax.all_gather(slab_keys, "seq", axis=0, tiled=True)
    source_values = lax.all_gather(slab_values, "seq", axis=0, tiled=True)
    fetch_slab_index = jnp.maximum(query_blocks[:, None] - offsets[None, :], 0)
    fetched = (gathered_keys, gathered_values, source_keys, source_values, fetch_slab_index)
    gathered_keys, gathered_values, source_keys, source_values, slab_index = fetched

    def as_blocks(array):
        return array.reshape(array.shape[0] // BLOCK, BLOCK, kv_count, DH).transpose(2, 0, 1, 3)

    cache_key_blocks = as_blocks(gathered_keys)
    cache_value_blocks = as_blocks(gathered_values)
    slab_key_blocks = as_blocks(source_keys)
    slab_value_blocks = as_blocks(source_values)
    rows_in_block = jnp.arange(BLOCK, dtype=jnp.int32)
    causal = rows_in_block[None, :] <= rows_in_block[:, None]
    slab_mask = slab_valid[:, None, :, None] & (
        (offsets[None, None, :, None] > 0) | causal[None, :, None, :]
    )
    slab_mask = slab_mask.reshape(blocks_here, BLOCK, WIN * BLOCK)
    full_mask = jnp.concatenate(
        [jnp.ones((blocks_here, BLOCK, listed * BLOCK), dtype=bool), slab_mask], axis=2
    )
    query_heads = arrived.reshape(blocks_here, BLOCK, head_count, DH).transpose(2, 0, 1, 3)
    score_scale = DH ** (-0.5)

    def attend(query_tile_rows, lists, head_number):
        kv_number = head_number // group_size
        cache_k = lax.dynamic_index_in_dim(cache_key_blocks, kv_number, 0, keepdims=False)
        cache_v = lax.dynamic_index_in_dim(cache_value_blocks, kv_number, 0, keepdims=False)
        slab_k = lax.dynamic_index_in_dim(slab_key_blocks, kv_number, 0, keepdims=False)
        slab_v = lax.dynamic_index_in_dim(slab_value_blocks, kv_number, 0, keepdims=False)
        selected_key_rows = jnp.concatenate(
            [
                jnp.take(cache_k, lists, axis=0).reshape(blocks_here, listed * BLOCK, DH),
                jnp.take(slab_k, slab_index, axis=0).reshape(blocks_here, WIN * BLOCK, DH),
            ],
            axis=1,
        )
        selected_value_rows = jnp.concatenate(
            [
                jnp.take(cache_v, lists, axis=0).reshape(blocks_here, listed * BLOCK, DH),
                jnp.take(slab_v, slab_index, axis=0).reshape(blocks_here, WIN * BLOCK, DH),
            ],
            axis=1,
        )
        logit_matrix = (
            jnp.einsum(
                "yav,ycv->yac",
                query_tile_rows,
                selected_key_rows,
                preferred_element_type=jnp.float32,
            )
            * score_scale
        )
        probability_weights = softmax_weights(logit_matrix, full_mask)
        weighted_total = jnp.einsum(
            "fgx,fxc->fgc",
            probability_weights,
            selected_value_rows,
            preferred_element_type=jnp.float32,
        )
        return weighted_total.astype(jnp.bfloat16)

    pair_count = head_count // 2

    def attend_pair(item):
        pair_queries, pair_lists, pair_numbers = item
        return jax.vmap(attend)(pair_queries, pair_lists, pair_numbers)

    results = lax.map(
        attend_pair,
        (
            query_heads.reshape(pair_count, 2, blocks_here, BLOCK, DH),
            block_lists.reshape(pair_count, 2, blocks_here, listed),
            jnp.arange(head_count, dtype=jnp.int32).reshape(pair_count, 2),
        ),
    )
    results = results.reshape(head_count, blocks_here, BLOCK, DH).transpose(1, 2, 0, 3)
    results = results.reshape(blocks_here * BLOCK, head_count * DH)
    return lax.all_to_all(results, "head", split_axis=0, concat_axis=1, tiled=True)


def solution(mesh):
    return jax.shard_map(
        per_device,
        mesh=mesh,
        in_specs=(
            P(("seq", "head"), None),
            P("seq", "head"),
            P("seq", "head"),
            P("seq", "head"),
            P("seq", "head"),
            P("head", "seq", None),
        ),
        out_specs=P(("seq", "head"), None),
        check_vma=False,
    )
```

profile of v0, /device:TPU:32, one launch (start us, length us, event | category | flops | bytes accessed | tf_op | source)
XLA Modules:
  0.0 750.2 jit_solution(7762240975053461179)
XLA Ops:
  9.3 1.9 copy.28
  11.2 16.8 %all-to-all-start = ((bf16[32,8,1024]{2,0,1:T(8,128)(2,1)}), bf16[32,8,1024]{2,0,1:T(8,128)(2,1)S(1)}, u32[]{:S(2)}, u32[]{:S(2)}) async-start(bf16[32,8,1024]{2,0,1:T(8,128)(2,1)} %bitcast.61), calls=%async_computation | async-start | bytes 1048576 | tf_op jit(solution)/shard_map/all_to_all | solution.py:28
  28.7 0.9 concatenate.26
  29.6 35.1 %all-to-all-done = bf16[32,8,1024]{2,0,1:T(8,128)(2,1)S(1)} async-done(((bf16[32,8,1024]{2,0,1:T(8,128)(2,1)}), bf16[32,8,1024]{2,0,1:T(8,128)(2,1)S(1)}, u32[]{:S(2)}, u32[]{:S(2)}) %all-to-all-start) | async-done | bytes 524320 | tf_op jit(solution)/shard_map/all_to_all | solution.py:28
  64.7 0.9 copy.21
  65.6 79.8 %all-gather.5.cloned.1.call-done = bf16[4096,128]{1,0:T(8,128)(2,1)} async-done(((bf16[64,128]{1,0:T(8,128)(2,1)}), bf16[4096,128]{1,0:T(8,128)(2,1)}) %all-gather.5.cloned.1.call-update) | async-done | bytes 1048592 | tf_op jit(solution)/shard_map/all_gather | solution.py:29
  145.4 119.9 %all-gather.9.cloned.1.call-done = bf16[4096,128]{1,0:T(8,128)(2,1)} async-done(((bf16[64,128]{1,0:T(8,128)(2,1)}), bf16[4096,128]{1,0:T(8,128)(2,1)}) %all-gather.9.cloned.1.call-update) | async-done | bytes 1048592 | tf_op jit(solution)/shard_map/all_gather | solution.py:30
  265.3 121.0 %all-gather.7.cloned.1.call-done = bf16[16384,128]{1,0:T(8,128)(2,1)} async-done(((bf16[256,128]{1,0:T(8,128)(2,1)}), bf16[16384,128]{1,0:T(8,128)(2,1)}) %all-gather.7.cloned.1.call-update) | async-done | bytes 4194320 | tf_op jit(solution)/shard_map/all_gather | solution.py:31
  386.3 120.4 %all-gather.11.cloned.1.call-done = bf16[16384,128]{1,0:T(8,128)(2,1)} async-done(((bf16[256,128]{1,0:T(8,128)(2,1)}), bf16[16384,128]{1,0:T(8,128)(2,1)}) %all-gather.11.cloned.1.call-update) | async-done | bytes 4194320 | tf_op jit(solution)/shard_map/all_gather | solution.py:32
  506.7 188.8 %while.14 = (s32[]{:T(128)}, bf16[4,2,4,64,128]{4,3,2,1,0:T(8,128)(2,1)}, pred[4,64,1792]{2,1,0:T(8,128)(4,1)}, bf16[4,2,4,64,128]{4,1,0,3,2:T(2,128)(2,1)}, bf1...) while((s32[]{:T(128)}, ...), condition=%wide.region_3.6_spmd.clone.clone, body=%wide.region_0.5_spmd.clone.clone.sunk | while | flops 494608064 | bytes 110837584 | solution.py:100
  506.7 7.8 %broadcast.365 = bf16[2,256,64,128]{3,2,1,0:T(8,128)(2,1)} broadcast(bf16[256,64,128]{2,1,0:T(8,128)(2,1)} %bitcast.104), dimensions={1,2,3} | broadcast | bytes 12582912 | tf_op jit(solution)/shard_map/while/body/eval_jaxpr/vmap(jit(dynamic_index_in_dim))/squeeze | solution.py:60
  514.7 4.0 gather_fusion
  518.8 7.8 %broadcast.366 = bf16[2,256,64,128]{3,2,1,0:T(8,128)(2,1)} broadcast(bf16[256,64,128]{2,1,0:T(8,128)(2,1)} %bitcast.106), dimensions={1,2,3} | broadcast | bytes 12582912 | tf_op jit(solution)/shard_map/while/body/eval_jaxpr/vmap(jit(dynamic_index_in_dim))/squeeze | solution.py:61
  526.6 4.1 gather_fusion.1
  530.7 1.2 copy_select_fusion.3
  532.6 3.6 gather_fusion.2
  536.8 3.7 gather_fusion.3
  540.5 3.3 broadcast_select_fusion.3
  543.7 1.0 constant_dynamic-slice_fusion.2
  544.8 1.6 multiply_select_fusion.2
  546.4 1.8 copy-done
  548.1 0.7 exponential_reduce_fusion.2
  548.9 5.0 fusion.38
  553.9 7.8 %broadcast.365 = bf16[2,256,64,128]{3,2,1,0:T(8,128)(2,1)} broadcast(bf16[256,64,128]{2,1,0:T(8,128)(2,1)} %bitcast.104), dimensions={1,2,3} | broadcast | bytes 12582912 | tf_op jit(solution)/shard_map/while/body/eval_jaxpr/vmap(jit(dynamic_index_in_dim))/squeeze | solution.py:60
  561.8 4.0 gather_fusion
  566.0 7.8 %broadcast.366 = bf16[2,256,64,128]{3,2,1,0:T(8,128)(2,1)} broadcast(bf16[256,64,128]{2,1,0:T(8,128)(2,1)} %bitcast.106), dimensions={1,2,3} | broadcast | bytes 12582912 | tf_op jit(solution)/shard_map/while/body/eval_jaxpr/vmap(jit(dynamic_index_in_dim))/squeeze | solution.py:61
  573.8 4.1 gather_fusion.1
  577.9 1.2 copy_select_fusion.3
  579.8 3.6 gather_fusion.2
  584.0 3.7 gather_fusion.3
  587.6 3.3 broadcast_select_fusion.3
  590.9 1.0 constant_dynamic-slice_fusion.2
  592.0 1.6 multiply_select_fusion.2
  593.5 1.8 copy-done
  595.3 0.7 exponential_reduce_fusion.2
  596.1 5.0 fusion.38
  601.1 7.8 %broadcast.365 = bf16[2,256,64,128]{3,2,1,0:T(8,128)(2,1)} broadcast(bf16[256,64,128]{2,1,0:T(8,128)(2,1)} %bitcast.104), dimensions={1,2,3} | broadcast | bytes 12582912 | tf_op jit(solution)/shard_map/while/body/eval_jaxpr/vmap(jit(dynamic_index_in_dim))/squeeze | solution.py:60
  609.0 4.0 gather_fusion
  613.1 7.8 %broadcast.366 = bf16[2,256,64,128]{3,2,1,0:T(8,128)(2,1)} broadcast(bf16[256,64,128]{2,1,0:T(8,128)(2,1)} %bitcast.106), dimensions={1,2,3} | broadcast | bytes 12582912 | tf_op jit(solution)/shard_map/while/body/eval_jaxpr/vmap(jit(dynamic_index_in_dim))/squeeze | solution.py:61
  621.0 4.1 gather_fusion.1
  625.1 1.2 copy_select_fusion.3
  627.0 3.6 gather_fusion.2
  631.2 3.7 gather_fusion.3
  634.8 3.3 broadcast_select_fusion.3
  638.1 1.0 constant_dynamic-slice_fusion.2
  639.1 1.6 multiply_select_fusion.2
  640.7 1.8 copy-done
  642.5 0.7 exponential_reduce_fusion.2
  643.3 5.0 fusion.38
  648.2 7.8 %broadcast.365 = bf16[2,256,64,128]{3,2,1,0:T(8,128)(2,1)} broadcast(bf16[256,64,128]{2,1,0:T(8,128)(2,1)} %bitcast.104), dimensions={1,2,3} | broadcast | bytes 12582912 | tf_op jit(solution)/shard_map/while/body/eval_jaxpr/vmap(jit(dynamic_index_in_dim))/squeeze | solution.py:60
  656.2 4.0 gather_fusion
  660.3 7.8 %broadcast.366 = bf16[2,256,64,128]{3,2,1,0:T(8,128)(2,1)} broadcast(bf16[256,64,128]{2,1,0:T(8,128)(2,1)} %bitcast.106), dimensions={1,2,3} | broadcast | bytes 12582912 | tf_op jit(solution)/shard_map/while/body/eval_jaxpr/vmap(jit(dynamic_index_in_dim))/squeeze | solution.py:61
  668.1 4.1 gather_fusion.1
  672.3 1.2 copy_select_fusion.3
  674.1 3.6 gather_fusion.2
  678.4 3.7 gather_fusion.3
  682.0 3.3 broadcast_select_fusion.3
  685.3 1.0 constant_dynamic-slice_fusion.2
  686.3 1.6 multiply_select_fusion.2
  687.9 1.8 copy-done
  690.4 5.0 fusion.38
  695.4 1.4 copy.29
  697.0 45.8 %all_to_all.35 = bf16[8,32,1024]{2,1,0:T(8,128)(2,1)S(1)} all-to-all(bf16[8,32,1024]{2,1,0:T(8,128)(2,1)S(1)} %all_to_all.29), channel_id=1, replica_groups=mesh['seq'=64,'head'=8] {'head'}, dimensions={0} | all-to-all | bytes 1048576 | tf_op jit(solution)/shard_map/all_to_all | solution.py:110
  742.8 0.8 copy.20
  (97 shorter events, 10.3 us)
Async XLA Ops:
  6.5 500.1 %copy-start.5 = (s32[8,4,24]{2,1,0:T(4,128)S(1)}, s32[8,4,24]{2,1,0:T(4,128)}, u32[]{:S(2)}) copy-start(s32[8,4,24]{2,1,0:T(4,128)} %param.17) | copy-start | bytes 9220
  6.5 138.8 %all-gather.5.cloned.1.call-start = ((), (), s32[]{:S(2)}) async-start(), calls=%async_computation.2 | async-start | bytes 1064960 | tf_op jit(solution)/shard_map/all_gather | solution.py:29
  7.3 258.0 %all-gather.9.cloned.1.call-start = ((), (), s32[]{:S(2)}) async-start(), calls=%async_computation.4 | async-start | bytes 1064960 | tf_op jit(solution)/shard_map/all_gather | solution.py:30
  8.0 378.3 %all-gather.7.cloned.1.call-start = ((), (), s32[]{:S(2)}) async-start(), calls=%async_computation.3 | async-start | bytes 4259840 | tf_op jit(solution)/shard_map/all_gather | solution.py:31
  8.7 497.9 %all-gather.11.cloned.1.call-start = ((), (), s32[]{:S(2)}) async-start(), calls=%async_computation.5 | async-start | bytes 4259840 | tf_op jit(solution)/shard_map/all_gather | solution.py:32
  11.2 53.5 %all-to-all-start = ((bf16[32,8,1024]{2,0,1:T(8,128)(2,1)}), bf16[32,8,1024]{2,0,1:T(8,128)(2,1)S(1)}, u32[]{:S(2)}, u32[]{:S(2)}) async-start(bf16[32,8,1024]{2,0,1:T(8,128)(2,1)} %bitcast.61), calls=%async_computation | async-start | bytes 1048576 | tf_op jit(solution)/shard_map/all_to_all | solution.py:28
  526.6 5.3 copy-start.1
  532.5 3.7 copy-start.2
  540.5 4.3 copy-start.3
  540.5 4.3 copy-start.4
  546.3 1.8 copy-start
  573.8 5.3 copy-start.1
  579.7 3.7 copy-start.2
  587.6 4.3 copy-start.3
  587.6 4.3 copy-start.4
  593.5 1.8 copy-start
  621.0 5.3 copy-start.1
  626.8 3.7 copy-start.2
  634.8 4.3 copy-start.3
  634.8 4.3 copy-start.4
  640.7 1.8 copy-start
  668.1 5.3 copy-start.1
  674.0 3.7 copy-start.2
  682.0 4.3 copy-start.3
  682.0 4.3 copy-start.4
  687.9 1.8 copy-start
Sparse Core Ops, SparseCore 0:
  9.5 135.8 all-gather.4
  147.5 117.7 all-gather.8
  267.5 118.7 all-gather.6
  388.3 118.3 all-gather.10
where the time goes:
time: 751 us; the launch traced here: 750 us
  waiting for transfers between devices  479 us (64%)
  local copies, waits for them, and re-layouts  147 us (20%)
  blocking collectives  45.8 us (6%)
  matrix products  26.2 us (3%)
  other arithmetic  21.6 us (3%)
  starting transfers between devices  16.9 us (2%)
  between operations  13.2 us (2%)
    all_gather x1, waiting for transfers between devices, per_device(): source_keys = lax.all_gather(slab_keys, 'seq', axis=0, tiled=True)  121 us
    all_gather x1, waiting for transfers between devices, per_device(): source_values = lax.all_gather(slab_values, 'seq', axis=0, tiled=True)  120 us
    all_gather x1, waiting for transfers between devices, per_device(): gathered_values = lax.all_gather(cache_values, 'seq', axis=0, tiled=True)  120 us
    all_gather x1, waiting for transfers between devices, per_device(): gathered_keys = lax.all_gather(cache_keys, 'seq', axis=0, tiled=True)  79.8 us
    all_to_all x1, blocking collectives, per_device(): lax.all_to_all(results, 'head', split_axis=0, concat_axis=1, tiled=True)  45.8 us
    all_to_all x1, waiting for transfers between devices, per_device(): lax.all_to_all(queries, 'head', split_axis=1, concat_axis=0, tiled=True)  35.1 us
    squeeze x4, local copies, waits for them, and re-layouts, attend(): lax.dynamic_index_in_dim(slab_value_blocks, kv_number, 0, keepdims=False)  31.3 us
    squeeze x4, local copies, waits for them, and re-layouts, attend(): lax.dynamic_index_in_dim(slab_key_blocks, kv_number, 0, keepdims=False)  31.3 us
  transfers between devices with their start and end apart: 5, of which 5 were waited for; matrix products, arithmetic and copies ran while one was open for 1% of the time, Pallas kernels for 0%

commit v1 on v0

--- a/solution.py
+++ b/solution.py
@@ -27,7 +27,9 @@
     slab_valid = query_blocks[:, None] - offsets[None, :] >= 0
     arrived = lax.all_to_all(queries, "head", split_axis=1, concat_axis=0, tiled=True)
     gathered_keys = lax.all_gather(cache_keys, "seq", axis=0, tiled=True)
-    gathered_values = lax.all_gather(cache_values, "seq", axis=0, tiled=True)
+    gathered_values = jnp.concatenate(
+        lax.all_to_all(jnp.stack([cache_values] * lax.axis_size("seq")), "seq", 0, 0), axis=0
+    )
     source_keys = lax.all_gather(slab_keys, "seq", axis=0, tiled=True)
     source_values = lax.all_gather(slab_values, "seq", axis=0, tiled=True)
     fetch_slab_index = jnp.maximum(query_blocks[:, None] - offsets[None, :], 0)

time: 751 us -> 648 us (0.86)
  waiting for transfers between devices: 479 us -> 325 us
  blocking collectives: 45.8 us -> 99 us
  starting transfers between devices: 16.9 us -> 8.44 us
    all_gather x1 -> x0, waiting for transfers between devices: 120 us -> none  [per_device(): gathered_values = lax.all_gather(cache_values, 'seq', axis=0, tiled=True)]
    all_to_all x0 -> x1, blocking collectives: none -> 53.2 us  [per_device(): lax.all_to_all(queries, 'head', split_axis=1, concat_axis=0, tiled=True)]
    all_to_all x1, waiting for transfers between devices: 35.1 us -> 0.01 us  [per_device(): lax.all_to_all(jnp.stack([cache_values] * lax.axis_size('seq')), 'seq', 0...]
    all_to_all x1, starting transfers between devices: 16.8 us -> 8.36 us  [per_device(): lax.all_to_all(jnp.stack([cache_values] * lax.axis_size('seq')), 'seq', 0...]
  transfers between devices with their start and end apart: 5 -> 4, of which waited for: 5 -> 3; matrix products, arithmetic and copies ran while one was open for 1% -> 1% of each run, Pallas kernels for 0% -> 0%
where the time goes in v1:
time: 648 us; the launch traced here: 647 us
  waiting for transfers between devices  325 us (50%)
  local copies, waits for them, and re-layouts  153 us (24%)
  blocking collectives  99 us (15%)
  matrix products  26.2 us (4%)
  other arithmetic  21.7 us (3%)
  between operations  13.2 us (2%)
  starting transfers between devices  8.44 us (1%)
    all_gather x1, waiting for transfers between devices, per_device(): source_keys = lax.all_gather(slab_keys, 'seq', axis=0, tiled=True)  127 us
    all_gather x1, waiting for transfers between devices, per_device(): source_values = lax.all_gather(slab_values, 'seq', axis=0, tiled=True)  121 us
    all_gather x1, waiting for transfers between devices, per_device(): gathered_keys = lax.all_gather(cache_keys, 'seq', axis=0, tiled=True)  74.8 us
    all_to_all x1, blocking collectives, per_device(): lax.all_to_all(queries, 'head', split_axis=1, concat_axis=0, tiled=True)  53.2 us
    all_to_all x1, blocking collectives, per_device(): lax.all_to_all(results, 'head', split_axis=0, concat_axis=1, tiled=True)  45.8 us
    squeeze x4, local copies, waits for them, and re-layouts, attend(): lax.dynamic_index_in_dim(slab_value_blocks, kv_number, 0, keepdims=False)  31.3 us
    squeeze x4, local copies, waits for them, and re-layouts, attend(): lax.dynamic_index_in_dim(slab_key_blocks, kv_number, 0, keepdims=False)  31.3 us
    dot_general x4, matrix products, attend(): jnp.einsum('fgx,fxc->fgc', probability_weights, selected_value_rows, pref...  19.9 us
  transfers between devices with their start and end apart: 4, of which 3 were waited for; matrix products, arithmetic and copies ran while one was open for 1% of the time, Pallas kernels for 0%

profile of v1, /device:TPU:32, one launch (start us, length us, event | category | flops | bytes accessed | tf_op | source)
XLA Modules:
  0.0 646.8 jit_solution(6135728305005097109)
XLA Ops:
  8.7 1.1 copy.28
  9.8 53.2 %all_to_all.40 = bf16[32,8,1024]{2,0,1:T(8,128)(2,1)S(1)} all-to-all(bf16[32,8,1024]{2,0,1:T(8,128)(2,1)S(1)} %bitcast.119), channel_id=1, replica_groups=mesh['seq'=64,'head'=8] {'head'}, dimensions={1} | all-to-all | bytes 1048576 | tf_op jit(solution)/shard_map/all_to_all | solution.py:28
  63.1 1.9 stack.2
  65.0 8.4 %all-to-all-start.1 = ((bf16[64,64,128]{2,1,0:T(8,128)(2,1)}), bf16[64,64,128]{2,1,0:T(8,128)(2,1)}, u32[]{:S(2)}, u32[]{:S(2)}) async-start(bf16[64,64,128]{2,1,0:T(8,128)(2,1)} %stack.2), calls=%async_computation.1 | async-start | bytes 2097152 | tf_op jit(solution)/shard_map/all_to_all | solution.py:31
  74.0 0.9 concatenate.26
  74.9 0.9 copy.21
  75.8 74.8 %all-gather.4.cloned.1.call-done = bf16[4096,128]{1,0:T(8,128)(2,1)} async-done(((bf16[64,128]{1,0:T(8,128)(2,1)}), bf16[4096,128]{1,0:T(8,128)(2,1)}) %all-gather.4.cloned.1.call-update) | async-done | bytes 1048592 | tf_op jit(solution)/shard_map/all_gather | solution.py:29
  150.7 127.3 %all-gather.6.cloned.1.call-done = bf16[16384,128]{1,0:T(8,128)(2,1)} async-done(((bf16[256,128]{1,0:T(8,128)(2,1)}), bf16[16384,128]{1,0:T(8,128)(2,1)}) %all-gather.6.cloned.1.call-update) | async-done | bytes 4194320 | tf_op jit(solution)/shard_map/all_gather | solution.py:33
  278.0 120.6 %all-gather.8.cloned.1.call-done = bf16[16384,128]{1,0:T(8,128)(2,1)} async-done(((bf16[256,128]{1,0:T(8,128)(2,1)}), bf16[16384,128]{1,0:T(8,128)(2,1)}) %all-gather.8.cloned.1.call-update) | async-done | bytes 4194320 | tf_op jit(solution)/shard_map/all_gather | solution.py:34
  398.5 193.5 %while.14 = (s32[]{:T(128)}, bf16[4,2,4,64,128]{4,3,2,1,0:T(8,128)(2,1)}, pred[4,64,1792]{2,1,0:T(8,128)(4,1)}, bf16[4,2,4,64,128]{4,1,0,3,2:T(2,128)(2,1)}, bf1...) while((s32[]{:T(128)}, ...), condition=%wide.region_3.6_spmd.clone.clone, body=%wide.region_0.5_spmd.clone.clone.sunk | while | flops 494608064 | bytes 106643248 | solution.py:102
  398.5 7.8 %broadcast.367 = bf16[2,256,64,128]{3,2,1,0:T(8,128)(2,1)} broadcast(bf16[256,64,128]{2,1,0:T(8,128)(2,1)} %bitcast.104), dimensions={1,2,3} | broadcast | bytes 12582912 | tf_op jit(solution)/shard_map/while/body/eval_jaxpr/vmap(jit(dynamic_index_in_dim))/squeeze | solution.py:62
  406.5 4.0 gather_fusion
  410.6 7.8 %broadcast.368 = bf16[2,256,64,128]{3,2,1,0:T(8,128)(2,1)} broadcast(bf16[256,64,128]{2,1,0:T(8,128)(2,1)} %bitcast.106), dimensions={1,2,3} | broadcast | bytes 12582912 | tf_op jit(solution)/shard_map/while/body/eval_jaxpr/vmap(jit(dynamic_index_in_dim))/squeeze | solution.py:63
  418.5 4.1 gather_fusion.1
  422.6 1.2 copy_select_fusion.3
  424.5 3.6 gather_fusion.2
  428.1 1.7 broadcast.370
  429.8 3.7 gather_fusion.3
  433.5 3.3 broadcast_select_fusion.3
  436.8 1.0 constant_dynamic-slice_fusion.2
  437.8 1.6 multiply_select_fusion.2
  439.4 1.8 copy-done
  441.9 5.0 fusion.38
  446.9 7.8 %broadcast.367 = bf16[2,256,64,128]{3,2,1,0:T(8,128)(2,1)} broadcast(bf16[256,64,128]{2,1,0:T(8,128)(2,1)} %bitcast.104), dimensions={1,2,3} | broadcast | bytes 12582912 | tf_op jit(solution)/shard_map/while/body/eval_jaxpr/vmap(jit(dynamic_index_in_dim))/squeeze | solution.py:62
  454.9 4.0 gather_fusion
  459.0 7.8 %broadcast.368 = bf16[2,256,64,128]{3,2,1,0:T(8,128)(2,1)} broadcast(bf16[256,64,128]{2,1,0:T(8,128)(2,1)} %bitcast.106), dimensions={1,2,3} | broadcast | bytes 12582912 | tf_op jit(solution)/shard_map/while/body/eval_jaxpr/vmap(jit(dynamic_index_in_dim))/squeeze | solution.py:63
  466.8 4.1 gather_fusion.1
  470.9 1.2 copy_select_fusion.3
  472.8 3.6 gather_fusion.2
  476.5 1.7 broadcast.370
  478.2 3.7 gather_fusion.3
  481.9 3.3 broadcast_select_fusion.3
  485.2 1.0 constant_dynamic-slice_fusion.2
  486.2 1.6 multiply_select_fusion.2
  487.8 1.8 copy-done
  490.3 5.0 fusion.38
  495.3 7.8 %broadcast.367 = bf16[2,256,64,128]{3,2,1,0:T(8,128)(2,1)} broadcast(bf16[256,64,128]{2,1,0:T(8,128)(2,1)} %bitcast.104), dimensions={1,2,3} | broadcast | bytes 12582912 | tf_op jit(solution)/shard_map/while/body/eval_jaxpr/vmap(jit(dynamic_index_in_dim))/squeeze | solution.py:62
  503.3 4.0 gather_fusion
  507.4 7.8 %broadcast.368 = bf16[2,256,64,128]{3,2,1,0:T(8,128)(2,1)} broadcast(bf16[256,64,128]{2,1,0:T(8,128)(2,1)} %bitcast.106), dimensions={1,2,3} | broadcast | bytes 12582912 | tf_op jit(solution)/shard_map/while/body/eval_jaxpr/vmap(jit(dynamic_index_in_dim))/squeeze | solution.py:63
  515.2 4.1 gather_fusion.1
  519.3 1.2 copy_select_fusion.3
  521.2 3.6 gather_fusion.2
  524.8 1.7 broadcast.370
  526.6 3.7 gather_fusion.3
  530.3 3.3 broadcast_select_fusion.3
  533.5 1.0 constant_dynamic-slice_fusion.2
  534.6 1.6 multiply_select_fusion.2
  536.2 1.8 copy-done
  538.7 5.0 fusion.38
  543.7 7.8 %broadcast.367 = bf16[2,256,64,128]{3,2,1,0:T(8,128)(2,1)} broadcast(bf16[256,64,128]{2,1,0:T(8,128)(2,1)} %bitcast.104), dimensions={1,2,3} | broadcast | bytes 12582912 | tf_op jit(solution)/shard_map/while/body/eval_jaxpr/vmap(jit(dynamic_index_in_dim))/squeeze | solution.py:62
  551.7 4.0 gather_fusion
  555.8 7.8 %broadcast.368 = bf16[2,256,64,128]{3,2,1,0:T(8,128)(2,1)} broadcast(bf16[256,64,128]{2,1,0:T(8,128)(2,1)} %bitcast.106), dimensions={1,2,3} | broadcast | bytes 12582912 | tf_op jit(solution)/shard_map/while/body/eval_jaxpr/vmap(jit(dynamic_index_in_dim))/squeeze | solution.py:63
  563.6 4.1 gather_fusion.1
  567.7 1.2 copy_select_fusion.3
  569.6 3.6 gather_fusion.2
  573.2 1.7 broadcast.370
  575.0 3.7 gather_fusion.3
  578.6 3.3 broadcast_select_fusion.3
  581.9 1.0 constant_dynamic-slice_fusion.2
  583.0 1.6 multiply_select_fusion.2
  584.5 1.8 copy-done
  587.1 5.0 fusion.38
  592.0 1.4 copy.29
  593.7 45.8 %all_to_all.41 = bf16[8,32,1024]{2,1,0:T(8,128)(2,1)S(1)} all-to-all(bf16[8,32,1024]{2,1,0:T(8,128)(2,1)S(1)} %all_to_all.33), channel_id=1, replica_groups=mesh['seq'=64,'head'=8] {'head'}, dimensions={0} | all-to-all | bytes 1048576 | tf_op jit(solution)/shard_map/all_to_all | solution.py:112
  (88 shorter events, 10.5 us)
Async XLA Ops:
  6.5 392.0 %copy-start.4 = (s32[8,4,24]{2,1,0:T(4,128)S(1)}, s32[8,4,24]{2,1,0:T(4,128)}, u32[]{:S(2)}) copy-start(s32[8,4,24]{2,1,0:T(4,128)} %param.17) | copy-start | bytes 9220
  6.5 144.1 %all-gather.4.cloned.1.call-start = ((), (), s32[]{:S(2)}) async-start(), calls=%async_computation.3 | async-start | bytes 1064960 | tf_op jit(solution)/shard_map/all_gather | solution.py:29
  7.3 270.7 %all-gather.6.cloned.1.call-start = ((), (), s32[]{:S(2)}) async-start(), calls=%async_computation.4 | async-start | bytes 4259840 | tf_op jit(solution)/shard_map/all_gather | solution.py:33
  8.0 390.5 %all-gather.8.cloned.1.call-start = ((), (), s32[]{:S(2)}) async-start(), calls=%async_computation.5 | async-start | bytes 4259840 | tf_op jit(solution)/shard_map/all_gather | solution.py:34
  65.0 85.7 %all-to-all-start.1 = ((bf16[64,64,128]{2,1,0:T(8,128)(2,1)}), bf16[64,64,128]{2,1,0:T(8,128)(2,1)}, u32[]{:S(2)}, u32[]{:S(2)}) async-start(bf16[64,64,128]{2,1,0:T(8,128)(2,1)} %stack.2), calls=%async_computation.1 | async-start | bytes 2097152 | tf_op jit(solution)/shard_map/all_to_all | solution.py:31
  418.4 5.3 copy-start.1
  433.5 4.3 copy-start.2
  433.5 4.3 copy-start.3
  439.4 1.8 copy-start
  466.8 5.3 copy-start.1
  481.9 4.3 copy-start.2
  481.9 4.3 copy-start.3
  487.8 1.8 copy-start
  515.2 5.3 copy-start.1
  530.3 4.3 copy-start.2
  530.3 4.3 copy-start.3
  536.1 1.8 copy-start
  563.6 5.3 copy-start.1
  578.6 4.3 copy-start.2
  578.6 4.3 copy-start.3
  584.5 1.8 copy-start
Sparse Core Ops, SparseCore 0:
  9.5 141.1 all-gather.3
  152.8 125.0 all-gather.5
  280.1 118.3 all-gather.7
